TPU v7x, 512 devices: a whole 4x8x8 slice. The times are simulated.
512 devices in a mesh: row: 32 (over y, x), col: 16 (over z, core).
Axes of the slice: x: 4, y: 8, z: 8, core: 2. Of those that a mesh axis runs over, the one named last changes fastest.
Arguments:
- source_features: bfloat16 [16, 2048, 256], P('col', 'row'), may hold values from -500 to 500
- target_features: bfloat16 [32768, 256], P(('row', 'col')), may hold values from -6 to 6
- weight: bfloat16 [256, 256], replicated, may hold values from -0.375 to 0.375
- score_source: float32 [4, 64], replicated, may hold values from -0.75 to 0.75
- score_target: float32 [4, 64], replicated, may hold values from -0.75 to 0.75
- out_bias: float32 [256], replicated, may hold values from -3 to 3
- block_list: int32 [32, 16, 48], P('row', 'col'), may hold values from 0 to 127, as said below
- block_count: int32 [32, 16], P('row', 'col'), may hold values from 8 to 48, as said below
- edge_bits: int32 [32, 16, 48, 16, 128], P('row', 'col'), may hold values from 0 to 255, as said below
Outputs:
- updated: bfloat16 [32768, 256], P(('row', 'col'))
Inputs may be any that keep to these rules, and one draw needn't show every extreme that they name: `block_list`: slot s of tile (r, c) names target block p // 16 and source block p % 16 of the tile; the first block_count[r, c] slots of a tile name distinct blocks and later slots are unused. `block_count`: some tile holds 48 blocks. `edge_bits`: bit b of entry [r, c, s, w, i] marks the edge from source 8 w + b to target i of the block in slot s. Some targets have no edge.
All inputs are finite; a program needn't handle non-finite values.
Results may differ from a plain program's by a relative error of at most 0.007.
The roundings to bfloat16 on the way count: a program that leaves them out, or rounds other values in their place, can miss the bound.
Values may be sent and summed in bfloat16 or wider, within the bound.
A program may use at most 64 MiB of HBM per device.

v0:
```python
import jax
import jax.numpy as jnp
from jax import lax
from jax.sharding import PartitionSpec as P

BLK = 128
SB = 16
very_low = -1e30
slope = 0.2


def unpack_all(packed):
    shifts = jnp.arange(8, dtype=jnp.int32)
    spread = jnp.right_shift(packed[:, :, None, :], shifts[None, None, :, None]) & 1
    return spread.reshape(packed.shape[0], packed.shape[1] * 8, packed.shape[2]) > 0


def all_scores(src_pick, dst_pick):
    raw = src_pick[:, :, :, None] + dst_pick[:, :, None, :]
    return jnp.where(raw > 0, raw, slope * raw)


def body(
    source_features,
    target_features,
    weight,
    score_source,
    score_target,
    out_bias,
    block_list,
    block_count,
    edge_bits,
):
    head_count = score_source.shape[0]
    head_size = score_source.shape[1]
    out_width = weight.shape[1]
    own_proj = jnp.dot(source_features[0], weight, preferred_element_type=jnp.float32).astype(
        jnp.bfloat16
    )
    projected = lax.all_gather(own_proj, "row", axis=0, tiled=True)
    src_logits = jnp.einsum(
        "nhk,hk->hn",
        projected.reshape(-1, head_count, head_size).astype(jnp.float32),
        score_source,
        precision=lax.Precision.HIGHEST,
    )
    dst_proj = jnp.dot(target_features, weight, preferred_element_type=jnp.float32)
    dst_local = jnp.einsum(
        "nhk,hk->hn",
        dst_proj.reshape(-1, head_count, head_size),
        score_target,
        precision=lax.Precision.HIGHEST,
    )
    dst_logits = lax.all_gather(dst_local, "col", axis=1, tiled=True)
    dst_rows = dst_logits.shape[1]
    dst_blocks_all = dst_rows // BLK
    src_blocks_all = src_logits.shape[1] // BLK
    slots = block_list[0, 0]
    live = block_count[0, 0]
    packed = edge_bits[0, 0]
    slot_count = slots.shape[0]
    dst_block = slots // SB
    src_block = slots % SB
    in_use = jnp.arange(slot_count, dtype=jnp.int32) < live
    edge_mask = unpack_all(packed) & in_use[:, None, None]
    src_pick = jnp.take(src_logits.reshape(head_count, src_blocks_all, BLK), src_block, axis=1)
    dst_pick = jnp.take(dst_logits.reshape(head_count, dst_blocks_all, BLK), dst_block, axis=1)
    owner = dst_block[:, None] == jnp.arange(dst_blocks_all, dtype=jnp.int32)[None, :]
    owner_float = owner.astype(jnp.float32)
    scores = all_scores(src_pick, dst_pick)
    block_max = jnp.max(jnp.where(edge_mask[None], scores, very_low), axis=2)
    spread_max = jnp.where(owner[None, :, :, None], block_max[:, :, None, :], very_low)
    row_max = jnp.max(spread_max, axis=1).reshape(head_count, dst_rows)
    row_max = lax.pmax(row_max, "col")
    prior_max = jnp.take(row_max.reshape(head_count, dst_blocks_all, BLK), dst_block, axis=1)
    scores = all_scores(src_pick, dst_pick)
    numer = jnp.exp(jnp.where(edge_mask[None], scores - prior_max[:, :, None, :], very_low))
    slot_denoms = jnp.sum(numer, axis=2)
    denoms = jnp.einsum(
        "sd,hsi->dih", owner_float, slot_denoms, precision=lax.Precision.HIGHEST
    ).reshape(dst_rows, head_count)
    weights = numer.astype(jnp.bfloat16)
    src_feats = jnp.take(
        projected.reshape(src_blocks_all, BLK, head_count, head_size), src_block, axis=0
    )
    product = jnp.einsum("hsji,sjhk->sihk", weights, src_feats, preferred_element_type=jnp.float32)
    accum = jnp.einsum(
        "sd,sihk->dihk", owner_float, product, precision=lax.Precision.HIGHEST
    ).reshape(dst_rows, out_width)
    accum, denoms = (
        lax.psum(accum.astype(jnp.bfloat16), "col").astype(jnp.float32),
        lax.psum(denoms.astype(jnp.bfloat16), "col").astype(jnp.float32),
    )
    own_count = dst_rows // lax.axis_size("col")
    first_row = lax.axis_index("col") * own_count
    accum = lax.dynamic_slice_in_dim(accum, first_row, own_count, 0)
    denoms = lax.dynamic_slice_in_dim(denoms, first_row, own_count, 0)
    own_count = accum.shape[0]
    blended = accum.reshape(own_count, head_count, head_size) / jnp.maximum(denoms, 1.0)[:, :, None]
    return jax.nn.elu(blended.reshape(own_count, out_width) + out_bias).astype(jnp.bfloat16)


def solution(mesh):
    placed = (
        P("col", "row", None),
        P(("row", "col"), None),
        P(),
        P(),
        P(),
        P(),
        P("row", "col", None),
        P("row", "col"),
        P("row", "col", None, None, None),
    )
    return jax.shard_map(
        body, mesh=mesh, in_specs=placed, out_specs=P(("row", "col"), None), check_vma=False
    )
```

profile of v0, /device:TPU:1, one launch (start us, length us, event | category | flops | bytes accessed | tf_op | source)
XLA Modules:
  0.0 296.6 jit_solution(9279656370350139183)
XLA Ops:
  6.5 0.0 copy-start
  6.5 0.0 all-gather.3.cloned.1.call-start
  6.5 0.9 copy-done
  7.4 1.5 convolution_convert_fusion
  9.0 0.0 all-gather.3.cloned.1.call-update
  9.0 0.0 all-reduce.2.cloned.1.call-start
  9.0 0.9 fusion.45
  9.9 0.1 reshape.177
  10.1 1.0 fusion.28
  11.1 24.6 %all-gather = f32[16,64,4]{1,2,0:T(4,128)S(1)} all-gather(f32[1,64,4]{1,2,0:T(4,128)S(1)} %bitcast.101), channel_id=1, replica_groups=mesh['row'=32,'col'=16] {'col'}, dimensions={0}, use_global_device_ids=true | all-gather | bytes 17408 | tf_op jit(solution)/shard_map/all_gather | solution.py:54
  35.6 0.1 reshape.217
  35.7 0.1 shift_right_arithmetic.30
  36.5 0.7 compare_and_fusion
  37.2 0.1 copy.42
  37.3 0.6 gather_fusion.2
  37.9 0.7 fusion.39
  38.6 1.9 fusion.17
  40.6 0.0 copy-start.2
  40.6 52.5 %all-gather.3.cloned.1.call-done = bf16[2048,256]{1,0:T(8,128)(2,1)} async-done(((bf16[64,256]{1,0:T(8,128)(2,1)}), bf16[2048,256]{1,0:T(8,128)(2,1)}) %all-gather.3.cloned.1.call-update) | async-done | bytes 1048592 | tf_op jit(solution)/shard_map/all_gather | solution.py:40
  93.1 1.6 copy.40
  94.7 1.2 fusion.44
  95.9 0.6 gather_fusion.1
  96.5 0.2 select_bitcast_fusion.1
  96.7 4.4 %select_reduce_fusion = f32[4,48,128]{2,0,1:T(4,128)S(1)} fusion(f32[4,48,128]{2,0,1:T(4,128)S(1)} %get-tuple-element.9, f32[4,48,128]{2,0,1:T(4,128)S(1)} %get-tuple-element.10, pred[48,128,128]{2,1,0:T(8,128)(4,1)S(1)} %fusion.17), kind=kLoop, calls=%fused_computation.6 | loop fusion | flops 18849792 | bytes 1081344 | tf_op jit(solution)/shard_map/reduce_max | solution.py:71
  101.1 0.1 select_reduce_fusion.1
  101.2 48.2 %pmax.7 = f32[4,8,128]{2,0,1:T(4,128)S(1)} all-reduce(f32[4,8,128]{2,0,1:T(4,128)S(1)} %copy.44), channel_id=1, replica_groups=mesh['row'=32,'col'=16] {'col'}, use_global_device_ids=true, to_apply=%region_2.4 | all-reduce | flops 4096 | bytes 32768 | tf_op jit(solution)/shard_map/pmax | solution.py:74
  149.4 0.6 gather_fusion.3
  150.1 0.0 copy-done.2
  150.1 0.8 select_bitcast_fusion
  150.8 0.0 copy-done.1
  150.8 0.8 reshape.228
  151.7 1.1 copy.39
  152.8 2.7 gather_fusion
  155.5 9.9 %fusion.18 = f32[48,128,4,64]{1,3,2,0:T(8,128)S(1)} fusion(f32[4,48,128]{2,0,1:T(4,128)S(1)} %copy-done.4, f32[4,48,128]{2,0,1:T(4,128)S(1)} %get-tuple-element.9, f32[4,48,128]{2,0,1:T(4,128)S(1)} %get-tuple-element.10, pred[48,128,128]{2,1,0:T(8,128)(4,1)S(1)} %copy-done.3, bf16[48,128,4,64]{1,3,2,0:T(8,128)(2,1)} %gather_fusion, ...), kind=kOutput, calls=%fused_computation.25 | convolution fusion | flops 426246144 | bytes 10518576 | tf_op jit(solution)/shard_map/hsji,sjhk->sihk/dot_general | solution.py:86
  165.4 0.0 copy-start.5
  165.4 5.7 %fusion.24 = bf16[8,128,4,64]{1,0,3,2:T(8,128)(2,1)S(1)} fusion(f32[48,128,4,64]{1,3,2,0:T(8,128)S(1)} %fusion.18, s32[48]{0:T(128)S(1)} %get-tuple-element.7), kind=kOutput, calls=%fused_computation.27 | convolution fusion | flops 151257472 | bytes 6815936 | tf_op jit(solution)/shard_map/sd,sihk->dihk/dot_general | solution.py:87
  171.1 0.1 copy.70
  171.2 1.0 copy.46
  172.2 0.0 all-reduce.2.cloned.1.call-update
  172.2 5.5 %fusion = f32[4,48,128]{2,0,1:T(4,128)S(1)} fusion(f32[4,48,128]{2,0,1:T(4,128)S(1)} %copy-done.4, f32[4,48,128]{2,0,1:T(4,128)S(1)} %get-tuple-element.9, f32[4,48,128]{2,0,1:T(4,128)S(1)} %get-tuple-element.10, pred[48,128,128]{2,1,0:T(8,128)(4,1)S(1)} %copy-done.3), kind=kLoop, calls=%fused_computation.7 | loop fusion | flops 21995520 | bytes 1179648 | tf_op jit(solution)/shard_map/reduce_sum | solution.py:78
  177.7 0.2 fusion.27
  177.9 27.0 %psum.15 = bf16[1024,4]{0,1:T(4,128)(2,1)S(1)} all-reduce(bf16[1024,4]{0,1:T(4,128)(2,1)S(1)} %bitcast.100), channel_id=1, replica_groups=mesh['row'=32,'col'=16] {'col'}, use_global_device_ids=true, to_apply=%region_5.7 | all-reduce | flops 4096 | bytes 16384 | tf_op jit(solution)/shard_map/psum | solution.py:92
  204.9 0.1 convert_maximum_fusion
  205.0 0.1 copy.48
  205.1 0.1 div.27
  205.2 0.1 div.28
  205.4 83.0 %all-reduce.2.cloned.1.call-done = bf16[1024,256]{1,0:T(8,128)(2,1)} async-done(((bf16[1024,256]{1,0:T(8,128)(2,1)}), bf16[1024,256]{1,0:T(8,128)(2,1)}) %all-reduce.2.cloned.1.call-update) | async-done | bytes 524304 | tf_op jit(solution)/shard_map/psum | solution.py:91
  288.3 1.4 fusion.32
  (17 shorter events, 0.1 us)
Async XLA Ops:
  6.5 0.9 copy-start
  6.5 86.5 %all-gather.3.cloned.1.call-start = ((), (), s32[]{:S(2)}) async-start(), calls=%async_computation | async-start | bytes 1081344 | tf_op jit(solution)/shard_map/all_gather | solution.py:40
  9.0 279.3 %all-reduce.2.cloned.1.call-start = ((), (), s32[]{:S(2)}) async-start(), calls=%async_computation.1 | async-start | bytes 1048576 | tf_op jit(solution)/shard_map/psum | solution.py:91
  40.6 109.5 %copy-start.2 = (pred[48,128,128]{2,1,0:T(8,128)(4,1)}, pred[48,128,128]{2,1,0:T(8,128)(4,1)S(1)}, u32[]{:S(2)}) copy-start(pred[48,128,128]{2,1,0:T(8,128)(4,1)S(1)} %fusion.17) | copy-start | bytes 2359300
  93.1 57.7 %copy-start.1 = (bf16[2048,256]{1,0:T(8,128)(2,1)S(1)}, bf16[2048,256]{1,0:T(8,128)(2,1)}, u32[]{:S(2)}) copy-start(bf16[2048,256]{1,0:T(8,128)(2,1)} %all-gather.3.cloned.1.call-done) | copy-start | bytes 3145732
  152.8 2.7 copy-start.3
  152.8 2.7 copy-start.4
  165.4 122.9 %copy-start.5 = (f32[256]{0:T(256)S(1)}, f32[256]{0:T(256)}, u32[]{:S(2)}) copy-start(f32[256]{0:T(256)} %param.16) | copy-start | bytes 3076
Sparse Core Ops, SparseCore 0:
  10.5 82.5 all-gather.2
  172.3 115.9 all-reduce.1
where the time goes:
time: 297 us
  waiting for transfers between devices  136 us (46%)
  blocking collectives  99.8 us (34%)
  matrix products  20.3 us (7%)
  other arithmetic  15.7 us (5%)
  between operations  14.3 us (5%)
  local copies, waits for them, and re-layouts  10.9 us (4%)
    psum x1, waiting for transfers between devices, body(): lax.psum(accum.astype(jnp.bfloat16), 'col').astype(jnp.float32)  83 us
    all_gather x1, waiting for transfers between devices, body(): projected = lax.all_gather(own_proj, 'row', axis=0, tiled=True)  52.5 us
    pmax x1, blocking collectives, body(): row_max = lax.pmax(row_max, 'col')  48.2 us
    psum x1, blocking collectives, body(): lax.psum(denoms.astype(jnp.bfloat16), 'col').astype(jnp.float32)  27 us
    all_gather x1, blocking collectives, body(): dst_logits = lax.all_gather(dst_local, 'col', axis=1, tiled=True)  24.6 us
    dot_general x1, matrix products, body(): jnp.einsum('hsji,sjhk->sihk', weights, src_feats, preferred_element_type=...  9.89 us
  transfers between devices with their start and end apart: 2, of which 2 were waited for; matrix products, arithmetic and copies ran while one was open for 4% of the time, Pallas kernels for 0%

commit v1 on v0

--- a/solution.py
+++ b/solution.py
@@ -2,6 +2,7 @@
 import jax.numpy as jnp
 from jax import lax
 from jax.sharding import PartitionSpec as P
+from jax.lax import all_to_all, axis_size
 
 BLK = 128
 SB = 16
@@ -37,7 +38,19 @@
     own_proj = jnp.dot(source_features[0], weight, preferred_element_type=jnp.float32).astype(
         jnp.bfloat16
     )
-    projected = lax.all_gather(own_proj, "row", axis=0, tiled=True)
+
+    def refer_the_columns(sample):
+        full_n = axis_size("row")
+        a_now = all_to_all(
+            jnp.tile(sample, list(map(lambda num: full_n if num == 0 else 1, range(sample.ndim)))),
+            "row",
+            split_axis=0,
+            concat_axis=0,
+            tiled=True,
+        )
+        return a_now
+
+    projected = refer_the_columns(own_proj)
     src_logits = jnp.einsum(
         "nhk,hk->hn",
         projected.reshape(-1, head_count, head_size).astype(jnp.float32),

time: 297 us -> 253 us (0.85)
  waiting for transfers between devices: 136 us -> 80.1 us
  starting transfers between devices: 0.04 us -> 10.5 us
    all_gather x1 -> x0, waiting for transfers between devices: 52.5 us -> none  [body(): projected = lax.all_gather(own_proj, 'row', axis=0, tiled=True)]
    all_to_all x0 -> x1, starting transfers between devices: none -> 10.5 us  [refer_the_columns(): all_to_all(jnp.tile(sample, list(map(lambda num: full_n if num == 0 else...]
  transfers between devices with their start and end apart: 2 -> 2, of which waited for: 2 -> 1; matrix products, arithmetic and copies ran while one was open for 4% -> 5% of each run, Pallas kernels for 0% -> 0%
where the time goes in v1:
time: 253 us; the launch traced here: 252 us
  blocking collectives  97.3 us (38%)
  waiting for transfers between devices  80.1 us (32%)
  matrix products  21.8 us (9%)
  other arithmetic  15.7 us (6%)
  between operations  14.3 us (6%)
  local copies, waits for them, and re-layouts  12.4 us (5%)
  starting transfers between devices  10.5 us (4%)
    psum x1, waiting for transfers between devices, body(): lax.psum(accum.astype(jnp.bfloat16), 'col').astype(jnp.float32)  80 us
    pmax x1, blocking collectives, body(): row_max = lax.pmax(row_max, 'col')  46.3 us
    psum x1, blocking collectives, body(): lax.psum(denoms.astype(jnp.bfloat16), 'col').astype(jnp.float32)  26.9 us
    all_gather x1, blocking collectives, body(): dst_logits = lax.all_gather(dst_local, 'col', axis=1, tiled=True)  24 us
    all_to_all x1, starting transfers between devices, refer_the_columns(): all_to_all(jnp.tile(sample, list(map(lambda num: full_n if num == 0 else...  10.5 us
    dot_general x1, matrix products, body(): jnp.einsum('hsji,sjhk->sihk', weights, src_feats, preferred_element_type=...  9.89 us
    dot_general x1, matrix products, body(): jnp.einsum('sd,sihk->dihk', owner_float, product, precision=lax.Precision...  5.67 us
    reduce_sum x1, other arithmetic, body(): slot_denoms = jnp.sum(numer, axis=2)  5.5 us
  transfers between devices with their start and end apart: 2, of which 1 were waited for; matrix products, arithmetic and copies ran while one was open for 5% of the time, Pallas kernels for 0%

profile of v1, /device:TPU:1, one launch (start us, length us, event | category | flops | bytes accessed | tf_op | source)
XLA Modules:
  0.0 252.1 jit_solution(1095672618639681363)
XLA Ops:
  6.5 0.0 copy-start
  6.5 0.9 copy-done
  7.4 0.9 convolution_convert_fusion
  8.3 1.1 tile.2
  9.5 10.5 %all-to-all-start = ((bf16[32,64,256]{2,1,0:T(8,128)(2,1)}), bf16[32,64,256]{2,1,0:T(8,128)(2,1)S(1)}, u32[]{:S(2)}, u32[]{:S(2)}) async-start(bf16[32,64,256]{2,1,0:T(8,128)(2,1)} %tile.2), calls=%async_computation | async-start | bytes 2097152 | tf_op jit(solution)/shard_map/all_to_all | solution.py:44
  20.0 0.0 all-reduce.2.cloned.1.call-start
  20.0 0.9 fusion.46
  20.9 0.1 reshape.186
  21.1 1.0 fusion.30
  22.0 24.0 %all-gather = f32[16,64,4]{1,2,0:T(4,128)S(1)} all-gather(f32[1,64,4]{1,2,0:T(4,128)S(1)} %bitcast.98), channel_id=1, replica_groups=mesh['row'=32,'col'=16] {'col'}, dimensions={0}, use_global_device_ids=true | all-gather | bytes 17408 | tf_op jit(solution)/shard_map/all_gather | solution.py:67
  46.1 0.1 reshape.226
  46.2 0.1 shift_right_arithmetic.30
  46.9 0.7 compare_and_fusion
  47.6 0.1 copy.40
  47.7 0.6 gather_fusion.2
  48.4 0.7 fusion.41
  49.0 1.9 fusion.17
  51.0 0.0 copy-start.1
  51.0 0.0 all-to-all-done
  51.0 1.9 reshape.238
  52.9 0.0 copy-done.5
  52.9 3.3 %fusion.23 = f32[4,1,2048]{2,1,0:T(1,128)S(1)} fusion(f32[4,64,1]{1,2,0:T(1,128)S(1)} %bitcast.100, bf16[2048,4,64]{2,1,0:T(4,128)(2,1)} %reshape.238), kind=kOutput, calls=%fused_computation.26 | convolution fusion | flops 6291456 | bytes 1082368 | tf_op jit(solution)/shard_map/nhk,hk->hn/dot_general | solution.py:54
  56.2 0.6 gather_fusion.1
  56.8 0.2 select_bitcast_fusion.1
  57.0 4.4 %select_reduce_fusion = f32[4,48,128]{2,0,1:T(4,128)S(1)} fusion(f32[4,48,128]{2,0,1:T(4,128)S(1)} %get-tuple-element.9, f32[4,48,128]{2,0,1:T(4,128)S(1)} %get-tuple-element.10, pred[48,128,128]{2,1,0:T(8,128)(4,1)S(1)} %fusion.17), kind=kLoop, calls=%fused_computation.6 | loop fusion | flops 18849792 | bytes 1081344 | tf_op jit(solution)/shard_map/reduce_max | solution.py:84
  61.4 0.1 select_reduce_fusion.1
  61.6 46.3 %pmax.7 = f32[4,8,128]{2,0,1:T(4,128)S(1)} all-reduce(f32[4,8,128]{2,0,1:T(4,128)S(1)} %copy.42), channel_id=1, replica_groups=mesh['row'=32,'col'=16] {'col'}, use_global_device_ids=true, to_apply=%region_2.4 | all-reduce | flops 4096 | bytes 32768 | tf_op jit(solution)/shard_map/pmax | solution.py:87
  107.9 0.6 gather_fusion.3
  108.6 0.8 select_bitcast_fusion
  109.3 0.8 reshape.237
  110.1 1.1 copy.37
  111.3 2.7 %gather_fusion = bf16[48,128,4,64]{1,3,2,0:T(8,128)(2,1)} fusion(bf16[16,128,4,64]{1,3,2,0:T(8,128)(2,1)S(1)} %copy.37, s32[1024]{0:T(1024)S(1)} %pad_clamp_fusion.1), kind=kCustom, calls=%fused_computation.2 | custom fusion | bytes 6291648 | tf_op jit(solution)/shard_map/jit(_take)/gather | solution.py:96
  114.0 0.0 copy-done.2
  114.0 9.9 %fusion.18 = f32[48,128,4,64]{1,3,2,0:T(8,128)S(1)} fusion(f32[4,48,128]{2,0,1:T(4,128)S(1)} %copy-done.3, f32[4,48,128]{2,0,1:T(4,128)S(1)} %get-tuple-element.9, f32[4,48,128]{2,0,1:T(4,128)S(1)} %get-tuple-element.10, pred[48,128,128]{2,1,0:T(8,128)(4,1)S(1)} %copy-done.2, bf16[48,128,4,64]{1,3,2,0:T(8,128)(2,1)} %gather_fusion, ...), kind=kOutput, calls=%fused_computation.25 | convolution fusion | flops 426246144 | bytes 10518576 | tf_op jit(solution)/shard_map/hsji,sjhk->sihk/dot_general | solution.py:99
  123.9 0.0 copy-start.4
  123.9 5.7 %fusion.26 = bf16[8,128,4,64]{1,0,3,2:T(8,128)(2,1)S(1)} fusion(f32[48,128,4,64]{1,3,2,0:T(8,128)S(1)} %fusion.18, s32[48]{0:T(128)S(1)} %get-tuple-element.7), kind=kOutput, calls=%fused_computation.29 | convolution fusion | flops 151257472 | bytes 6815936 | tf_op jit(solution)/shard_map/sd,sihk->dihk/dot_general | solution.py:100
  129.6 0.1 copy.71
  129.7 1.0 copy.44
  130.7 0.0 all-reduce.2.cloned.1.call-update
  130.7 5.5 %fusion = f32[4,48,128]{2,0,1:T(4,128)S(1)} fusion(f32[4,48,128]{2,0,1:T(4,128)S(1)} %copy-done.3, f32[4,48,128]{2,0,1:T(4,128)S(1)} %get-tuple-element.9, f32[4,48,128]{2,0,1:T(4,128)S(1)} %get-tuple-element.10, pred[48,128,128]{2,1,0:T(8,128)(4,1)S(1)} %copy-done.2), kind=kLoop, calls=%fused_computation.7 | loop fusion | flops 21995520 | bytes 1179648 | tf_op jit(solution)/shard_map/reduce_sum | solution.py:91
  136.2 0.2 fusion.29
  136.4 26.9 %psum.15 = bf16[1024,4]{0,1:T(4,128)(2,1)S(1)} all-reduce(bf16[1024,4]{0,1:T(4,128)(2,1)S(1)} %bitcast.97), channel_id=1, replica_groups=mesh['row'=32,'col'=16] {'col'}, use_global_device_ids=true, to_apply=%region_5.7 | all-reduce | flops 4096 | bytes 16384 | tf_op jit(solution)/shard_map/psum | solution.py:105
  163.3 0.1 convert_maximum_fusion
  163.4 0.1 copy.46
  163.5 0.1 div.27
  163.6 0.1 div.28
  163.8 80.0 %all-reduce.2.cloned.1.call-done = bf16[1024,256]{1,0:T(8,128)(2,1)} async-done(((bf16[1024,256]{1,0:T(8,128)(2,1)}), bf16[1024,256]{1,0:T(8,128)(2,1)}) %all-reduce.2.cloned.1.call-update) | async-done | bytes 524304 | tf_op jit(solution)/shard_map/psum | solution.py:104
  243.8 1.4 fusion.34
  (17 shorter events, 0.1 us)
Async XLA Ops:
  6.5 0.9 copy-start
  6.5 46.3 %copy-start.5 = (f32[4,64]{1,0:T(4,128)S(1)}, f32[4,64]{1,0:T(4,128)}, u32[]{:S(2)}) copy-start(f32[4,64]{1,0:T(4,128)} %param.14) | copy-start | bytes 3076
  9.5 41.5 %all-to-all-start = ((bf16[32,64,256]{2,1,0:T(8,128)(2,1)}), bf16[32,64,256]{2,1,0:T(8,128)(2,1)S(1)}, u32[]{:S(2)}, u32[]{:S(2)}) async-start(bf16[32,64,256]{2,1,0:T(8,128)(2,1)} %tile.2), calls=%async_computation | async-start | bytes 2097152 | tf_op jit(solution)/shard_map/all_to_all | solution.py:44
  20.0 223.8 %all-reduce.2.cloned.1.call-start = ((), (), s32[]{:S(2)}) async-start(), calls=%async_computation.1 | async-start | bytes 1048576 | tf_op jit(solution)/shard_map/psum | solution.py:104
  51.0 57.6 %copy-start.1 = (pred[48,128,128]{2,1,0:T(8,128)(4,1)}, pred[48,128,128]{2,1,0:T(8,128)(4,1)S(1)}, u32[]{:S(2)}) copy-start(pred[48,128,128]{2,1,0:T(8,128)(4,1)S(1)} %fusion.17) | copy-start | bytes 2359300
  111.2 2.7 %copy-start.2 = (pred[48,128,128]{2,1,0:T(8,128)(4,1)S(1)}, pred[48,128,128]{2,1,0:T(8,128)(4,1)}, u32[]{:S(2)}) copy-start(pred[48,128,128]{2,1,0:T(8,128)(4,1)} %copy-done.1) | copy-start | bytes 2359300
  111.2 2.7 %copy-start.3 = (f32[4,48,128]{2,0,1:T(4,128)S(1)}, f32[4,48,128]{2,0,1:T(4,128)}, u32[]{:S(2)}) copy-start(f32[4,48,128]{2,0,1:T(4,128)} %select_bitcast_fusion) | copy-start | bytes 294916
  123.9 119.9 %copy-start.4 = (f32[256]{0:T(256)S(1)}, f32[256]{0:T(256)}, u32[]{:S(2)}) copy-start(f32[256]{0:T(256)} %param.16) | copy-start | bytes 3076
Sparse Core Ops, SparseCore 0:
  130.8 112.9 all-reduce.1
